TPU v7x, 32 devices: a whole 2x2x4 slice. The times are simulated.
32 devices in a mesh: dp: 4 (over y, x), mp: 8 (over z, core).
Axes of the slice: x: 2, y: 2, z: 4, core: 2. Of those that a mesh axis runs over, the one named last changes fastest.
Arguments:
- hidden_in: bfloat16 [512, 8192], P('dp', 'mp'), may hold values from -256 to 256
- out_grad: bfloat16 [512, 8192], P('dp', 'mp'), may hold values from -1.796875 to 1.796875
- neighbours: bfloat16 [80, 128, 1536], P('dp', 'mp'), may hold values from -6 to 6
- counts: int32 [8], P('dp'), may hold values from 2 to 10, as said below
- slot_owner: int32 [80], P('dp'), may hold values from -1 to 79, as said below
- w_query: bfloat16 [8192, 4096], P(None, 'mp'), may hold values from -0.0625 to 0.0625
- w_key: bfloat16 [1536, 4096], P(None, 'mp'), may hold values from -0.15625 to 0.15625
- w_value: bfloat16 [1536, 4096], P(None, 'mp'), may hold values from -0.15625 to 0.15625
- w_out: bfloat16 [4096, 8192], P('mp'), may hold values from -0.59765625 to 0.59765625
Outputs:
- layer_out: bfloat16 [512, 8192], P('dp', 'mp')
- neighbour_grad: bfloat16 [80, 128, 1536], P('dp', 'mp')
Inputs may be any that keep to these rules, and one draw needn't show every extreme that they name: `counts`: every draw has one decoder group (spans g * 2 to g * 2 + 1) whose spans all have 10 neighbours. `slot_owner`: entry i is the span slot c * 10 + j that encoder slot i fills, or -1 for an empty encoder slot. Each slot with j < counts[c] is named exactly once, no other slot is named. The 20 entries of one index of dp name at most 5 slots of the spans of one decoder group (spans g * 2 to g * 2 + 1), and in every draw some index of dp names exactly 5 for some group.
All inputs are finite; a program needn't handle non-finite values.
Results may differ from a plain program's by a relative error of at most 0.024.
Values may be sent and summed in bfloat16 or wider, within the bound.
A program may use at most 128 MiB of HBM per device.

v0:
```python
import math

import jax
import jax.numpy as jnp
from jax import lax
from jax.sharding import PartitionSpec as P

DH = 128
MAXN = 10


def per_device(hidden_in, out_grad, neighbours, counts, slot_owner, w_query, w_key, w_value, w_out):
    groups = lax.axis_size("dp")
    spans = counts.shape[0]
    slots_group = spans * MAXN
    src_slots = slot_owner.shape[0]
    capacity = src_slots // groups
    rows_dev = neighbours.shape[1]
    enc_width = neighbours.shape[2]
    neigh_len = rows_dev * lax.axis_size("mp")
    heads_dev = w_query.shape[1] // DH
    query_width = w_query.shape[1]
    score_scale = 1.0 / math.sqrt(DH)
    contract_last = (((1,), (1,)), ((), ()))
    x_all, dy_all = (
        lax.all_gather(hidden_in, "mp", axis=1, tiled=True),
        lax.all_gather(out_grad, "mp", axis=1, tiled=True),
    )
    tokens_dev = x_all.shape[0]
    span_len = tokens_dev // spans
    queries = jnp.dot(x_all, w_query, preferred_element_type=jnp.float32).astype(jnp.bfloat16)
    grad_attended = lax.dot_general(
        dy_all, w_out, contract_last, preferred_element_type=jnp.float32
    ).astype(jnp.bfloat16)
    slot_order = jnp.arange(src_slots, dtype=jnp.int32)
    dest_group = jnp.where(slot_owner >= 0, slot_owner // slots_group, -1)
    earlier = (dest_group[None, :] == dest_group[:, None]) & (
        slot_order[None, :] < slot_order[:, None]
    )
    rank_in = jnp.sum(earlier.astype(jnp.int32), axis=1)
    position = jnp.where(slot_owner >= 0, dest_group * capacity + rank_in, -1)
    picked = position[None, :] == slot_order[:, None]
    source = jnp.sum(jnp.where(picked, slot_order[None, :], 0), axis=1)
    filled = jnp.any(picked, axis=1)
    send_rows = jnp.where(
        filled[:, None, None], jnp.take(neighbours, source, axis=0), jnp.zeros((), jnp.bfloat16)
    )
    send_rows = send_rows.reshape(groups, capacity, rows_dev, enc_width)
    send_tags = jnp.where(filled, jnp.take(slot_owner, source), -1).reshape(groups, capacity)
    got_rows, got_tags = (
        lax.all_to_all(send_rows, "dp", split_axis=0, concat_axis=0, tiled=True),
        lax.all_to_all(send_tags, "dp", split_axis=0, concat_axis=0, tiled=True),
    )
    got_rows = got_rows.reshape(src_slots, rows_dev, enc_width)
    got_tags = got_tags.reshape(src_slots)
    got_valid = got_tags >= 0
    local_slot = jnp.where(got_valid, got_tags % slots_group, -1)
    wanted = jnp.arange(slots_group, dtype=jnp.int32)
    matches = local_slot[None, :] == wanted[:, None]
    chosen = jnp.sum(jnp.where(matches, slot_order[None, :], 0), axis=1)
    safe_slot = jnp.maximum(local_slot, 0)
    gathered = lax.all_gather(got_rows, "mp", axis=1, tiled=True)
    encoded = jnp.take(gathered, chosen, axis=0)
    flat_rows = encoded.reshape(slots_group * neigh_len, enc_width)
    key_rows = jnp.dot(flat_rows, w_key, preferred_element_type=jnp.float32).astype(jnp.bfloat16)
    value_rows = jnp.dot(flat_rows, w_value, preferred_element_type=jnp.float32).astype(
        jnp.bfloat16
    )
    key_rows = key_rows.reshape(spans, MAXN * neigh_len, heads_dev, DH)
    value_rows = value_rows.reshape(spans, MAXN * neigh_len, heads_dev, DH)
    query_blocks = queries.reshape(spans, span_len, heads_dev, DH)
    grad_blocks = grad_attended.reshape(spans, span_len, heads_dev, DH)
    key_slot = jnp.arange(MAXN * neigh_len, dtype=jnp.int32) // neigh_len
    live_keys = key_slot[None, :] < counts[:, None]
    scores = (
        jnp.einsum("cqhd,ckhd->chqk", query_blocks, key_rows, preferred_element_type=jnp.float32)
        * score_scale
    )
    scores = jnp.where(live_keys[:, None, None, :], scores, -jnp.inf)
    peak_score = jnp.max(scores, axis=-1, keepdims=True)
    exponent = jnp.exp(scores - peak_score)
    weights = exponent / jnp.sum(exponent, axis=-1, keepdims=True)
    weights_bf = weights.astype(jnp.bfloat16)
    attended = jnp.einsum(
        "chqk,ckhd->cqhd", weights_bf, value_rows, preferred_element_type=jnp.float32
    ).astype(jnp.bfloat16)
    grad_values = jnp.einsum(
        "chqk,cqhd->ckhd", weights_bf, grad_blocks, preferred_element_type=jnp.float32
    ).astype(jnp.bfloat16)
    grad_weights = jnp.einsum(
        "cqhd,ckhd->chqk", grad_blocks, value_rows, preferred_element_type=jnp.float32
    )
    inner_sum = jnp.sum(weights * grad_weights, axis=-1, keepdims=True)
    grad_scores = (weights * (grad_weights - inner_sum) * score_scale).astype(jnp.bfloat16)
    grad_keys = jnp.einsum(
        "chqk,cqhd->ckhd", grad_scores, query_blocks, preferred_element_type=jnp.float32
    ).astype(jnp.bfloat16)
    out_part = jnp.dot(
        attended.reshape(tokens_dev, query_width), w_out, preferred_element_type=jnp.float32
    )
    grad_enc = lax.dot_general(
        grad_keys.reshape(-1, query_width), w_key, contract_last, preferred_element_type=jnp.float32
    )
    grad_enc = grad_enc + lax.dot_general(
        grad_values.reshape(-1, query_width),
        w_value,
        contract_last,
        preferred_element_type=jnp.float32,
    )
    grad_enc = grad_enc.reshape(slots_group, neigh_len, enc_width)
    spread = jnp.where(got_valid[:, None, None], jnp.take(grad_enc, safe_slot, axis=0), 0.0)
    out_sum, grad_sum = (
        lax.psum_scatter(
            out_part.astype(jnp.bfloat16), "mp", scatter_dimension=1, tiled=True
        ).astype(jnp.float32),
        lax.psum_scatter(spread.astype(jnp.bfloat16), "mp", scatter_dimension=1, tiled=True).astype(
            jnp.float32
        ),
    )
    grad_rows = grad_sum.astype(jnp.bfloat16)
    returned = lax.all_to_all(
        grad_rows.reshape(groups, capacity, rows_dev, enc_width),
        "dp",
        split_axis=0,
        concat_axis=0,
        tiled=True,
    )
    returned = returned.reshape(src_slots, rows_dev, enc_width)
    neighbour_grad = jnp.where(
        (slot_owner >= 0)[:, None, None],
        jnp.take(returned, jnp.maximum(position, 0), axis=0),
        jnp.zeros((), jnp.bfloat16),
    )
    layer_out = out_sum.astype(jnp.bfloat16)
    return (layer_out, neighbour_grad)


def solution(mesh):
    return jax.shard_map(
        per_device,
        mesh=mesh,
        in_specs=(
            P("dp", "mp"),
            P("dp", "mp"),
            P("dp", "mp", None),
            P("dp"),
            P("dp"),
            P(None, "mp"),
            P(None, "mp"),
            P(None, "mp"),
            P("mp", None),
        ),
        out_specs=(P("dp", "mp"), P("dp", "mp", None)),
        check_vma=False,
    )
```

profile of v0, /device:TPU:0, one launch (start us, length us, event | category | flops | bytes accessed | tf_op | source)
XLA Modules:
  0.0 391.9 jit_solution(2107015490624368091)
XLA Ops:
  10.4 1.8 gather_fusion.3
  12.6 18.7 %all_to_all.16 = bf16[4,5,16,1536]{3,2,1,0:T(8,128)(2,1)} all-to-all(bf16[4,5,16,1536]{3,2,1,0:T(8,128)(2,1)S(1)} %bitcast.66), channel_id=1, replica_groups=mesh['dp'=4,'mp'=8] {'dp'}, dimensions={0} | all-to-all | bytes 1966080 | tf_op jit(solution)/shard_map/all_to_all | solution.py:51
  32.8 3.2 all-to-all-start
  36.2 4.4 %all-to-all-done = s32[4,1,5]{2,1,0:T(1,128)S(1)} async-done(((s32[4,1,5]{2,1,0:T(1,128)}), s32[4,1,5]{2,1,0:T(1,128)S(1)}, u32[]{:S(2)}, u32[]{:S(2)}) %all-to-all-start) | async-done | bytes 112 | tf_op jit(solution)/shard_map/all_to_all | solution.py:52
  41.5 5.3 %convolution_convert_fusion.6 = bf16[128,512]{1,0:T(8,128)(2,1)S(1)} fusion(bf16[128,8192]{1,0:T(8,128)(2,1)} %all-gather.6.cloned.1.call-done, bf16[8192,512]{1,0:T(8,128)(2,1)} %param.16), kind=kOutput, calls=%fused_computation.41 | convolution fusion | flops 1073807360 | bytes 10616832 | tf_op jit(solution)/shard_map/dot_general | solution.py:31
  46.8 24.9 %all-gather.8.cloned.1.call-done = bf16[128,8192]{1,0:T(8,128)(2,1)} async-done(((bf16[128,1024]{1,0:T(8,128)(2,1)}), bf16[128,8192]{1,0:T(8,128)(2,1)}) %all-gather.8.cloned.1.call-update) | async-done | bytes 2097168 | tf_op jit(solution)/shard_map/all_gather | solution.py:27
  71.7 6.9 %convolution_convert_fusion.5 = bf16[128,512]{1,0:T(8,128)(2,1)S(1)} fusion(bf16[128,8192]{1,0:T(8,128)(2,1)} %all-gather.8.cloned.1.call-done, bf16[512,8192]{1,0:T(8,128)(2,1)} %param.19), kind=kOutput, calls=%fused_computation.40 | convolution fusion | flops 1073807360 | bytes 10616832 | tf_op jit(solution)/shard_map/dot_general | solution.py:32
  78.7 71.9 %all-gather.4.cloned.1.call-done = bf16[20,128,1536]{2,1,0:T(8,128)(2,1)} async-done(((bf16[20,16,1536]{2,1,0:T(8,128)(2,1)}), bf16[20,128,1536]{2,1,0:T(8,128)(2,1)}) %all-gather.4.cloned.1.call-update) | async-done | bytes 7864336 | tf_op jit(solution)/shard_map/all_gather | solution.py:62
  150.6 8.8 %gather_fusion.1 = bf16[20,128,1536]{2,1,0:T(8,128)(2,1)} fusion(bf16[20,128,1536]{2,1,0:T(8,128)(2,1)} %all-gather.4.cloned.1.call-done, s32[1024]{0:T(1024)S(1)} %pad_clamp_fusion.2), kind=kCustom, calls=%fused_computation.3 | custom fusion | bytes 15728720 | tf_op jit(solution)/shard_map/jit(_take)/gather | solution.py:63
  159.4 7.2 %bitcast_select_fusion = bf16[2560,1536]{1,0:T(8,128)(2,1)} fusion(bf16[20,128,1536]{2,1,0:T(8,128)(2,1)} %gather_fusion.1, pred[2560]{0:T(1024)(128)(4,1)S(1)} %broadcast_bitcast_fusion), kind=kLoop, calls=%fused_computation.10 | loop fusion | flops 3932160 | bytes 15731200 | tf_op jit(solution)/shard_map/jit(_take)/select_n | solution.py:63
  166.6 8.8 %convolution_convert_fusion.2 = bf16[2560,512]{1,0:T(8,128)(2,1)} fusion(bf16[2560,1536]{1,0:T(8,128)(2,1)} %bitcast_select_fusion, bf16[1536,512]{1,0:T(8,128)(2,1)S(1)} %copy-done.6), kind=kOutput, calls=%fused_computation.12 | convolution fusion | flops 4027842560 | bytes 12058624 | tf_op jit(solution)/shard_map/dot_general | solution.py:66
  175.5 5.0 %reshape.272 = bf16[2,1280,4,128]{3,2,1,0:T(4,128)(2,1)} reshape(bf16[2560,512]{1,0:T(8,128)(2,1)} %convolution_convert_fusion.2) | data formatting | bytes 5242880 | tf_op jit(solution)/shard_map/reshape | solution.py:70
  180.4 8.8 %convolution_convert_fusion.1 = bf16[2560,512]{1,0:T(8,128)(2,1)} fusion(bf16[2560,1536]{1,0:T(8,128)(2,1)} %bitcast_select_fusion, bf16[1536,512]{1,0:T(8,128)(2,1)S(1)} %copy-done), kind=kOutput, calls=%fused_computation.11 | convolution fusion | flops 4027842560 | bytes 12058624 | tf_op jit(solution)/shard_map/dot_general | solution.py:65
  189.3 4.9 %reshape.274 = bf16[2,1280,4,128]{3,2,1,0:T(4,128)(2,1)} reshape(bf16[2560,512]{1,0:T(8,128)(2,1)} %convolution_convert_fusion.1) | data formatting | bytes 5242880 | tf_op jit(solution)/shard_map/reshape | solution.py:69
  194.2 2.8 fusion.6
  196.9 1.9 fusion.52
  200.6 2.6 fusion.18
  203.1 5.1 %fusion.8 = bf16[2,1280,4,128]{1,3,2,0:T(8,128)(2,1)} fusion(bf16[2,64,4,128]{3,2,1,0:T(4,128)(2,1)S(1)} %reshape.276, f32[2,4,64]{2,1,0:T(4,128)S(1)} %get-tuple-element.8, f32[2,4,64,1280]{3,2,1,0:T(8,128)} %copy-done.4), kind=kOutput, calls=%fused_computation.22 | convolution fusion | flops 171050752 | bytes 5376000 | tf_op jit(solution)/shard_map/chqk,cqhd->ckhd/dot_general | solution.py:87
  208.3 8.1 %fusion.7 = bf16[2,1280,4,128]{1,3,2,0:T(8,128)(2,1)} fusion(f32[2,4,64,1280]{3,2,1,0:T(8,128)} %fusion.18, bf16[2,64,4,128]{3,2,1,0:T(4,128)(2,1)S(1)} %reshape.273, f32[2,4,64,1280]{3,2,1,0:T(8,128)} %get-tuple-element.9, f32[2,4,64]{2,1,0:T(4,128)S(1)} %get-tuple-element.8), kind=kOutput, calls=%fused_computation.21 | convolution fusion | flops 173672192 | bytes 7997440 | tf_op jit(solution)/shard_map/chqk,cqhd->ckhd/dot_general | solution.py:95
  216.3 5.3 %copy.51 = bf16[2,1280,4,128]{3,2,1,0:T(4,128)(2,1)} copy(bf16[2,1280,4,128]{1,3,2,0:T(8,128)(2,1)} %fusion.7) | data formatting | bytes 5242880 | tf_op jit(solution)/shard_map/convert_element_type | solution.py:97
  221.6 9.6 %fusion.13 = f32[2560,1536]{1,0:T(8,128)} fusion(bf16[1536,512]{1,0:T(8,128)(2,1)S(1)} %copy-done, bf16[320,8,4,128]{3,2,1,0:T(4,128)(2,1)} %bitcast.70), kind=kOutput, calls=%fused_computation.27 | convolution fusion | flops 4026531840 | bytes 19922944 | tf_op jit(solution)/shard_map/dot_general | solution.py:101
  231.2 5.4 %copy.53 = bf16[2,1280,4,128]{3,2,1,0:T(4,128)(2,1)} copy(bf16[2,1280,4,128]{1,3,2,0:T(8,128)(2,1)} %fusion.8) | data formatting | bytes 5242880 | tf_op jit(solution)/shard_map/convert_element_type | solution.py:89
  236.7 10.6 %convolution_add_fusion = bf16[2560,1536]{1,0:T(8,128)(2,1)} fusion(f32[2560,1536]{1,0:T(8,128)} %fusion.13, bf16[1536,512]{1,0:T(8,128)(2,1)S(1)} %copy-done.7, bf16[320,8,4,128]{3,2,1,0:T(4,128)(2,1)} %bitcast.69), kind=kOutput, calls=%fused_computation.8 | convolution fusion | flops 4034396160 | bytes 27787264 | tf_op jit(solution)/shard_map/dot_general | solution.py:104
  247.3 8.5 %gather_fusion.2 = bf16[20,128,1536]{2,1,0:T(8,128)(2,1)} fusion(bf16[20,128,1536]{2,1,0:T(8,128)(2,1)} %bitcast.65, s32[1024]{0:T(1024)S(1)} %pad_clamp_fusion.1), kind=kCustom, calls=%fused_computation.4 | custom fusion | bytes 15728720 | tf_op jit(solution)/shard_map/jit(_take)/gather | solution.py:111
  255.8 9.4 %select_convert_fusion = bf16[20,128,1536]{2,1,0:T(8,128)(2,1)} fusion(bf16[20,128,1536]{2,1,0:T(8,128)(2,1)} %gather_fusion.2, pred[20]{0:T(512)(128)(4,1)S(1)} %get-tuple-element.5, pred[20]{0:T(512)(128)(4,1)S(1)} %ge.65), kind=kLoop, calls=%fused_computation.7 | loop fusion | flops 7864320 | bytes 15728680 | tf_op jit(solution)/shard_map/convert_element_type | solution.py:116
  265.3 4.5 %fusion.28 = bf16[2,64,4,128]{3,1,2,0:T(8,128)(2,1)S(1)} fusion(bf16[2,1280,4,128]{3,2,1,0:T(4,128)(2,1)} %reshape.272, f32[2,4,64]{2,1,0:T(4,128)S(1)} %get-tuple-element.8, f32[2,4,64,1280]{3,2,1,0:T(8,128)} %copy-done.4), kind=kOutput, calls=%fused_computation.42 | convolution fusion | flops 169805568 | bytes 5376000 | tf_op jit(solution)/shard_map/chqk,ckhd->cqhd/dot_general | solution.py:84
  269.9 6.2 %convolution_convert_fusion = bf16[128,8192]{1,0:T(8,128)(2,1)} fusion(bf16[512,8192]{1,0:T(8,128)(2,1)} %param.19, bf16[16,8,4,128]{3,2,1,0:T(4,128)(2,1)S(1)} %bitcast.72), kind=kOutput, calls=%fused_computation.9 | convolution fusion | flops 1074790400 | bytes 10616832 | tf_op jit(solution)/shard_map/dot_general | solution.py:98
  276.1 72.5 %reduce-scatter.5.cloned.1.call-done = bf16[20,16,1536]{2,1,0:T(8,128)(2,1)} async-done(((bf16[20,128,1536]{2,1,0:T(8,128)(2,1)}), bf16[20,16,1536]{2,1,0:T(8,128)(2,1)}) %reduce-scatter.5.cloned.1.call-update) | async-done | bytes 983056 | tf_op jit(solution)/shard_map/reduce_scatter | solution.py:116
  348.6 3.8 all-to-all-start.2
  352.4 10.9 %all-to-all-done.2 = bf16[4,5,16,1536]{3,2,1,0:T(8,128)(2,1)S(1)} async-done(((bf16[4,5,16,1536]{3,2,1,0:T(8,128)(2,1)}), bf16[4,5,16,1536]{3,2,1,0:T(8,128)(2,1)S(1)}, u32[]{:S(2)}, u32[]{:S(2)}) %all-to-all-start.2) | async-done | bytes 983072 | tf_op jit(solution)/shard_map/all_to_all | solution.py:121
  363.9 1.2 select_select_fusion
  365.1 20.3 %reduce-scatter.3.cloned.1.call-done = bf16[128,1024]{1,0:T(8,128)(2,1)} async-done(((bf16[128,8192]{1,0:T(8,128)(2,1)}), bf16[128,1024]{1,0:T(8,128)(2,1)}) %reduce-scatter.3.cloned.1.call-update) | async-done | bytes 262160 | tf_op jit(solution)/shard_map/reduce_scatter | solution.py:113
  (65 shorter events, 8.6 us)
Async XLA Ops:
  7.2 173.3 %copy-start = (bf16[1536,512]{1,0:T(8,128)(2,1)S(1)}, bf16[1536,512]{1,0:T(8,128)(2,1)}, u32[]{:S(2)}) copy-start(bf16[1536,512]{1,0:T(8,128)(2,1)} %param.17) | copy-start | bytes 4718596
  7.2 34.3 %all-gather.6.cloned.1.call-start = ((), (), s32[]{:S(2)}) async-start(), calls=%async_computation.6 | async-start | bytes 2359296 | tf_op jit(solution)/shard_map/all_gather | solution.py:26
  7.9 63.8 %all-gather.8.cloned.1.call-start = ((), (), s32[]{:S(2)}) async-start(), calls=%async_computation.8 | async-start | bytes 2359296 | tf_op jit(solution)/shard_map/all_gather | solution.py:27
  8.7 141.9 %all-gather.4.cloned.1.call-start = ((), (), s32[]{:S(2)}) async-start(), calls=%async_computation.5 | async-start | bytes 8847360 | tf_op jit(solution)/shard_map/all_gather | solution.py:62
  12.2 19.3 %copy-start.2 = (s32[20]{0:T(128)S(1)}, s32[20]{0:T(128)}, u32[]{:S(2)}) copy-start(s32[20]{0:T(128)} %param.15) | copy-start | bytes 244
  12.3 23.8 %copy-start.5 = (s32[2]{0:T(128)S(1)}, s32[2]{0:T(128)}, u32[]{:S(2)}) copy-start(s32[2]{0:T(128)} %param.14) | copy-start | bytes 28
  32.8 7.8 %all-to-all-start = ((s32[4,1,5]{2,1,0:T(1,128)}), s32[4,1,5]{2,1,0:T(1,128)S(1)}, u32[]{:S(2)}, u32[]{:S(2)}) async-start(s32[4,1,5]{2,1,0:T(1,128)} %bitcast.2), calls=%async_computation | async-start | bytes 4096 | tf_op jit(solution)/shard_map/all_to_all | solution.py:52
  36.1 312.5 %reduce-scatter.5.cloned.1.call-start = ((), (), s32[]{:S(2)}) async-start(), calls=%async_computation.9 | async-start | bytes 8847360 | tf_op jit(solution)/shard_map/reduce_scatter | solution.py:116
  159.4 7.2 %copy-start.6 = (bf16[1536,512]{1,0:T(8,128)(2,1)S(1)}, bf16[1536,512]{1,0:T(8,128)(2,1)}, u32[]{:S(2)}) copy-start(bf16[1536,512]{1,0:T(8,128)(2,1)} %param.18) | copy-start | bytes 4718596
  196.9 2.7 copy-start.4
  196.9 3.6 copy-start.3
  231.2 5.4 %copy-start.7 = (bf16[1536,512]{1,0:T(8,128)(2,1)S(1)}, bf16[1536,512]{1,0:T(8,128)(2,1)}, u32[]{:S(2)}) copy-start(bf16[1536,512]{1,0:T(8,128)(2,1)} %param.18) | copy-start | bytes 4718596
  265.3 120.1 %reduce-scatter.3.cloned.1.call-start = ((), (), s32[]{:S(2)}) async-start(), calls=%async_computation.7 | async-start | bytes 2359296 | tf_op jit(solution)/shard_map/reduce_scatter | solution.py:113
  348.6 36.8 %copy-start.1 = (bf16[1536,512]{1,0:T(8,128)(2,1)S(1)}, bf16[1536,512]{1,0:T(8,128)(2,1)}, u32[]{:S(2)}) copy-start(bf16[1536,512]{1,0:T(8,128)(2,1)} %param.17) | copy-start | bytes 4718596
  348.6 14.7 %all-to-all-start.2 = ((bf16[4,5,16,1536]{3,2,1,0:T(8,128)(2,1)}), bf16[4,5,16,1536]{3,2,1,0:T(8,128)(2,1)S(1)}, u32[]{:S(2)}, u32[]{:S(2)}) async-start(bf16[4,5,16,1536]{3,2,1,0:T(8,128)(2,1)} %bitcast.71), calls=%async_computation.4 | async-start | bytes 1966080 | tf_op jit(solution)/shard_map/all_to_all | solution.py:121
Sparse Core Ops, SparseCore 0:
  9.6 31.7 all-gather.5
  43.1 28.6 all-gather.7
  73.3 77.2 all-gather.3
  265.4 83.1 reduce-scatter.4
  351.3 33.9 reduce-scatter.2
where the time goes:
time: 393 us; the launch traced here: 392 us
  waiting for transfers between devices  206 us (52%)
  matrix products  79.4 us (20%)
  local copies, waits for them, and re-layouts  43.6 us (11%)
  other arithmetic  22.6 us (6%)
  blocking collectives  18.7 us (5%)
  between operations  14 us (4%)
  starting transfers between devices  7.2 us (2%)
    reduce_scatter x1, waiting for transfers between devices, per_device(): lax.psum_scatter(spread.astype(jnp.bfloat16), 'mp', scatter_dimension=1,...  72.5 us
    all_gather x1, waiting for transfers between devices, per_device(): gathered = lax.all_gather(got_rows, 'mp', axis=1, tiled=True)  71.9 us
    all_gather x1, waiting for transfers between devices, per_device(): lax.all_gather(out_grad, 'mp', axis=1, tiled=True)  24.9 us
    reduce_scatter x1, waiting for transfers between devices, per_device(): lax.psum_scatter(out_part.astype(jnp.bfloat16), 'mp', scatter_dimension=1...  20.3 us
    all_to_all x1, blocking collectives, per_device(): lax.all_to_all(send_rows, 'dp', split_axis=0, concat_axis=0, tiled=True)  18.7 us
    all_to_all x1, waiting for transfers between devices, per_device(): lax.all_to_all(grad_rows.reshape(groups, capacity, rows_dev, enc_width),...  10.9 us
    dot_general x1, matrix products, per_device(): lax.dot_general(grad_values.reshape(-1, query_width), w_value, contract_l...  10.6 us
    dot_general x1, matrix products, per_device(): lax.dot_general(grad_keys.reshape(-1, query_width), w_key, contract_last,...  9.62 us
  transfers between devices with their start and end apart: 7, of which 7 were waited for; matrix products, arithmetic and copies ran while one was open for 8% of the time, Pallas kernels for 0%

commit v1 on v0

v1 whole, which is shorter than its diff:
```python
import functools
import math

import jax
import jax.numpy as jnp
from jax import lax
from jax.experimental import pallas as pl
from jax.experimental.pallas import tpu as pltpu
from jax.sharding import PartitionSpec as P

DH = 128
MAXN = 10
MESH = pl.DeviceIdType.MESH
NT = (((1,), (1,)), ((), ()))
TN = (((0,), (0,)), ((), ()))
VMEM_LIMIT = 62 * 1024 * 1024


def dot_f32(a, b, dims=(((1,), (0,)), ((), ()))):
    return lax.dot_general(a, b, dims, preferred_element_type=jnp.float32)


def greet(peers):
    barrier = pltpu.get_barrier_semaphore()
    total = 0
    for cond, dev in peers:
        if cond is None:
            pl.semaphore_signal(barrier, inc=1, device_id=dev, device_id_type=MESH)
            total = total + 1
        else:

            @pl.when(cond)
            def _(dev=dev):
                pl.semaphore_signal(barrier, inc=1, device_id=dev, device_id_type=MESH)

            total = total + jnp.where(cond, 1, 0)
    pl.semaphore_wait(barrier, total)


def forward_kernel(
    n_dp,
    n_mp,
    capacity,
    xd_in,
    rows_in,
    tags_in,
    counts_in,
    wq_in,
    wk_in,
    wv_in,
    wo_in,
    att_out,
    gk_out,
    gv_out,
    xd,
    nb,
    tags,
    wq,
    wk,
    wv,
    wo,
    keys,
    vals,
    queries,
    grads,
    bias,
    w_sem,
    a2a_send,
    a2a_recv,
    tag_send,
    tag_recv,
    own_sem,
    xd_send,
    xd_recv,
    nb_send,
    nb_recv,
):
    dp = lax.axis_index("dp")
    mp = lax.axis_index("mp")
    n_z = n_mp // 2
    z = mp // 2
    core = mp % 2
    partner = {"mp": mp + 1 - 2 * core}
    up = {"mp": lax.rem(mp + 2, n_mp)}
    down = {"mp": lax.rem(mp + n_mp - 2, n_mp)}
    has_up = z < n_z - 1
    has_down = z > 0
    block = nb.shape[1] // n_dp
    tokens = att_out.shape[0]
    feat = xd.shape[2]

    def peer(k):
        return lax.rem(dp + k, n_dp)

    weight_copies = [
        pltpu.make_async_copy(src, dst, w_sem.at[i])
        for i, (src, dst) in enumerate(((wq_in, wq), (wo_in, wo), (wk_in, wk), (wv_in, wv)))
    ]

    def line(buf, send, recv, origin, direction):
        slot = origin * 2 + core
        return pltpu.make_async_remote_copy(
            src_ref=buf.at[slot],
            dst_ref=buf.at[slot],
            send_sem=send.at[direction, origin],
            recv_sem=recv.at[slot],
            device_id=(up, down, partner)[direction],
            device_id_type=MESH,
        )

    def arrived(buf, send, recv, slot):
        pltpu.make_async_remote_copy(
            src_ref=buf.at[slot],
            dst_ref=buf.at[slot],
            send_sem=send.at[0, 0],
            recv_sem=recv.at[slot],
            device_id=partner,
            device_id_type=MESH,
        ).wait_recv()

    def send_own(args):
        @pl.when(has_up)
        def _():
            line(*args, z, 0).start()

        @pl.when(has_down)
        def _():
            line(*args, z, 1).start()

        line(*args, z, 2).start()

    def relay(args, s):
        @pl.when(z - s >= 0)
        def _():
            arrived(*args, (z - s) * 2 + core)

            @pl.when(has_up)
            def _():
                line(*args, z - s, 0).start()

            line(*args, z - s, 2).start()

        @pl.when(z + s <= n_z - 1)
        def _():
            arrived(*args, (z + s) * 2 + core)

            @pl.when(has_down)
            def _():
                line(*args, z + s, 1).start()

            line(*args, z + s, 2).start()

    def drain(args):
        def step(origin, carry):
            @pl.when(jnp.logical_and(origin <= z, has_up))
            def _():
                line(*args, origin, 0).wait_send()

            @pl.when(jnp.logical_and(origin >= z, has_down))
            def _():
                line(*args, origin, 1).wait_send()

            line(*args, origin, 2).wait_send()
            return carry

        lax.fori_loop(0, n_z, step, 0)

    xd_args = (xd, xd_send, xd_recv)
    nb_args = (nb, nb_send, nb_recv)

    own_xd = pltpu.make_async_copy(xd_in, xd.at[mp], own_sem.at[0])
    own_rows = pltpu.make_async_copy(
        rows_in.at[dp], nb.at[mp, pl.ds(dp * block, block)], own_sem.at[1]
    )
    own_tags = pltpu.make_async_copy(tags_in.at[dp], tags.at[dp], own_sem.at[2])
    own_xd.start()
    own_rows.start()
    own_tags.start()
    greet(
        [(None, {"dp": peer(k)}) for k in range(1, n_dp)]
        + [(None, partner), (has_up, up), (has_down, down)]
    )

    def row_copy(k):
        to = peer(k)
        return pltpu.make_async_remote_copy(
            src_ref=rows_in.at[to],
            dst_ref=nb.at[mp, pl.ds(dp * block, block)],
            send_sem=a2a_send.at[k],
            recv_sem=a2a_recv.at[k],
            device_id={"dp": to},
            device_id_type=MESH,
        )

    def tag_copy(k):
        to = peer(k)
        return pltpu.make_async_remote_copy(
            src_ref=tags_in.at[to],
            dst_ref=tags.at[dp],
            send_sem=tag_send.at[k],
            recv_sem=tag_recv.at[k],
            device_id={"dp": to},
            device_id_type=MESH,
        )

    for k in range(1, n_dp):
        row_copy(k).start()
    for k in range(1, n_dp):
        tag_copy(k).start()
    own_xd.wait()
    send_own(xd_args)
    for copy in weight_copies:
        copy.start()
    own_rows.wait()
    for k in range(1, n_dp):
        row_copy(k).wait()
    send_own(nb_args)
    own_tags.wait()
    for k in range(1, n_dp):
        tag_copy(k).wait()

    def xd_step(s, carry):
        relay(xd_args, s)
        return carry

    lax.fori_loop(1, n_z, xd_step, 0)

    def project(slot):
        rows = nb[slot]
        keys[slot] = dot_f32(rows, wk[...]).astype(jnp.bfloat16)
        vals[slot] = dot_f32(rows, wv[...]).astype(jnp.bfloat16)

    def both_cores(origin):
        arrived(*nb_args, origin * 2 + 1 - core)

        def step(c, carry):
            project(origin * 2 + c)
            return carry

        lax.fori_loop(0, 2, step, 0)

    def nb_step(s, carry):
        relay(nb_args, s)

        @pl.when(s == 1)
        def _():
            for copy in weight_copies:
                copy.wait()

            def other(origin, c):
                arrived(*xd_args, origin * 2 + 1 - core)
                return c

            lax.fori_loop(0, n_z, other, 0)

            def add(m, c):
                q, g = c
                cols = pl.ds(pl.multiple_of(m * feat, feat), feat)
                q = q + dot_f32(xd[m, :tokens, :], wq[cols, :])
                g = g + dot_f32(xd[m, tokens:, :], wo[:, cols], NT)
                return (q, g)

            zero = jnp.zeros(queries.shape, jnp.float32)
            q, g = lax.fori_loop(0, n_mp, add, (zero, zero))
            queries[...] = q.astype(jnp.bfloat16)
            grads[...] = g.astype(jnp.bfloat16)
            both_cores(z)

        @pl.when(z - s >= 0)
        def _():
            both_cores(z - s)

        @pl.when(z + s <= n_z - 1)
        def _():
            both_cores(z + s)

        return carry

    lax.fori_loop(1, n_z, nb_step, 0)

    span_len = tokens // (counts_in.shape[0])
    lane = lax.broadcasted_iota(jnp.int32, (1, tokens), 1)
    spans = counts_in.shape[0]
    first = jnp.zeros((1, tokens), jnp.int32)
    limit = jnp.zeros((1, tokens), jnp.int32)
    for c in range(spans):
        here = jnp.logical_and(lane >= c * span_len, lane < (c + 1) * span_len)
        first = jnp.where(here, (dp * spans + c) * MAXN, first)
        limit = jnp.where(here, counts_in[c : c + 1, :], limit)
    width = block // capacity
    for g in range(n_dp):
        for i in range(capacity):
            tag = tags[g, i : i + 1, :]
            place = tag - first
            live = jnp.logical_and(tag >= 0, jnp.logical_and(place >= 0, place < limit))
            value = jnp.where(live, 0.0, -jnp.inf)
            low = (g * capacity + i) * width
            bias[low : low + width, :] = jnp.broadcast_to(value, (width, tokens))

    scale = 1.0 / math.sqrt(DH)
    shard = nb.shape[1]
    total = n_mp * shard
    for h in range(queries.shape[1] // DH):
        cols = slice(h * DH, (h + 1) * DH)
        q = queries[:, cols]
        g = grads[:, cols]
        k = keys[:, :, cols].reshape(total, DH)
        v = vals[:, :, cols].reshape(total, DH)
        scores = dot_f32(k, q, NT) * scale
        scores = (scores.reshape(n_mp, shard, tokens) + bias[...][None]).reshape(total, tokens)
        peak = jnp.max(scores, axis=0, keepdims=True)
        expo = jnp.exp(scores - peak)
        weights = expo * (1.0 / jnp.sum(expo, axis=0, keepdims=True))
        weights_bf = weights.astype(jnp.bfloat16)
        att_out[:, cols] = dot_f32(weights_bf, v, TN).astype(jnp.bfloat16)
        gv_out[:, :, cols] = dot_f32(weights_bf, g).astype(jnp.bfloat16).reshape(n_mp, shard, DH)
        grad_w = dot_f32(v, g, NT)
        inner = jnp.sum(weights * grad_w, axis=0, keepdims=True)
        grad_s = (weights * (grad_w - inner) * scale).astype(jnp.bfloat16)
        gk_out[:, :, cols] = dot_f32(grad_s, q).astype(jnp.bfloat16).reshape(n_mp, shard, DH)

    drain(xd_args)
    drain(nb_args)


def forward(xd_shard, send_rows, send_tags, counts_rows, w_query, w_key, w_value, w_out, n_dp, n_mp):
    capacity = send_tags.shape[1]
    tokens = xd_shard.shape[0] // 2
    send_tags = jnp.broadcast_to(
        jnp.pad(send_tags, ((0, 0), (0, -capacity % 8)), constant_values=-1)[:, :, None],
        (n_dp, capacity + (-capacity % 8), tokens),
    )
    shard = n_dp * send_rows.shape[1]
    enc = send_rows.shape[2]
    width = w_query.shape[1]

    bf = jnp.bfloat16
    n_z = n_mp // 2
    hbm = pl.BlockSpec(memory_space=pl.ANY)
    vm = pl.BlockSpec(memory_space=pltpu.VMEM)
    dma = pltpu.SemaphoreType.DMA
    return pl.pallas_call(
        functools.partial(forward_kernel, n_dp, n_mp, capacity),
        out_shape=(
            jax.ShapeDtypeStruct((tokens, width), bf),
            jax.ShapeDtypeStruct((n_mp, shard, width), bf),
            jax.ShapeDtypeStruct((n_mp, shard, width), bf),
        ),
        in_specs=[hbm, hbm, hbm, vm, hbm, hbm, hbm, hbm],
        out_specs=(vm, vm, vm),
        scratch_shapes=[
            pltpu.VMEM((n_mp,) + xd_shard.shape, bf),
            pltpu.VMEM((n_mp, shard, enc), bf),
            pltpu.VMEM(send_tags.shape, jnp.int32),
            pltpu.VMEM(w_query.shape, bf),
            pltpu.VMEM(w_key.shape, bf),
            pltpu.VMEM(w_value.shape, bf),
            pltpu.VMEM(w_out.shape, bf),
            pltpu.VMEM((n_mp, shard, width), bf),
            pltpu.VMEM((n_mp, shard, width), bf),
            pltpu.VMEM((tokens, width), bf),
            pltpu.VMEM((tokens, width), bf),
            pltpu.VMEM((shard, tokens), jnp.float32),
            dma((4,)),
            dma((n_dp,)),
            dma((n_dp,)),
            dma((n_dp,)),
            dma((n_dp,)),
            dma((3,)),
            dma((3, n_z)),
            dma((n_mp,)),
            dma((3, n_z)),
            dma((n_mp,)),
        ],
        compiler_params=pltpu.CompilerParams(
            collective_id=0, has_side_effects=True, vmem_limit_bytes=VMEM_LIMIT
        ),
        name="gather_attend",
    )(xd_shard, send_rows, send_tags, counts_rows, w_query, w_key, w_value, w_out)


def per_device(hidden_in, out_grad, neighbours, counts, slot_owner, w_query, w_key, w_value, w_out):
    groups = lax.axis_size("dp")
    n_mp = lax.axis_size("mp")
    spans = counts.shape[0]
    slots_group = spans * MAXN
    src_slots = slot_owner.shape[0]
    capacity = src_slots // groups
    rows_dev = neighbours.shape[1]
    enc_width = neighbours.shape[2]
    query_width = w_query.shape[1]
    slot_order = jnp.arange(src_slots, dtype=jnp.int32)
    dest_group = jnp.where(slot_owner >= 0, slot_owner // slots_group, -1)
    earlier = (dest_group[None, :] == dest_group[:, None]) & (
        slot_order[None, :] < slot_order[:, None]
    )
    rank_in = jnp.sum(earlier.astype(jnp.int32), axis=1)
    position = jnp.where(slot_owner >= 0, dest_group * capacity + rank_in, -1)
    picked = position[None, :] == slot_order[:, None]
    source = jnp.sum(jnp.where(picked, slot_order[None, :], 0), axis=1)
    filled = jnp.any(picked, axis=1)
    send_rows = jnp.where(
        filled[:, None, None], jnp.take(neighbours, source, axis=0), jnp.zeros((), jnp.bfloat16)
    )
    send_rows = send_rows.reshape(groups, capacity * rows_dev, enc_width)
    send_tags = jnp.sum(
        jnp.where(picked, slot_owner[None, :] + 1, 0), axis=1
    ).reshape(groups, capacity) - 1
    counts_rows = jnp.broadcast_to(counts[:, None], (spans, hidden_in.shape[0]))
    attended, grad_keys, grad_values = forward(
        jnp.concatenate([hidden_in, out_grad], axis=0),
        send_rows,
        send_tags,
        counts_rows,
        w_query,
        w_key,
        w_value,
        w_out,
        groups,
        n_mp,
    )
    grad_enc = lax.dot_general(
        grad_keys.reshape(-1, query_width), w_key, NT, preferred_element_type=jnp.float32
    )
    grad_enc = grad_enc + lax.dot_general(
        grad_values.reshape(-1, query_width), w_value, NT, preferred_element_type=jnp.float32
    )
    out_part = jnp.dot(attended, w_out, preferred_element_type=jnp.float32)
    grad_rows = lax.psum_scatter(
        grad_enc.astype(jnp.bfloat16), "mp", scatter_dimension=0, tiled=True
    )
    layer_out = lax.psum_scatter(
        out_part.astype(jnp.bfloat16), "mp", scatter_dimension=1, tiled=True
    )
    returned = lax.all_to_all(
        grad_rows.reshape(groups, capacity, rows_dev, enc_width),
        "dp",
        split_axis=0,
        concat_axis=0,
        tiled=True,
    )
    returned = returned.reshape(src_slots, rows_dev, enc_width)
    neighbour_grad = jnp.where(
        (slot_owner >= 0)[:, None, None],
        jnp.take(returned, jnp.maximum(position, 0), axis=0),
        jnp.zeros((), jnp.bfloat16),
    )
    return (layer_out, neighbour_grad)


def solution(mesh):
    return jax.shard_map(
        per_device,
        mesh=mesh,
        in_specs=(
            P("dp", "mp"),
            P("dp", "mp"),
            P("dp", "mp", None),
            P("dp"),
            P("dp"),
            P(None, "mp"),
            P(None, "mp"),
            P(None, "mp"),
            P("mp", None),
        ),
        out_specs=(P("dp", "mp"), P("dp", "mp", None)),
        check_vma=False,
    )
```

time: 393 us -> 284 us (0.72)
  Pallas kernels: 0 us -> 117 us
  waiting for transfers between devices: 206 us -> 111 us
  matrix products: 79.4 us -> 27.9 us
  local copies, waits for them, and re-layouts: 43.6 us -> 3.47 us
  blocking collectives: 18.7 us -> 0 us
  other arithmetic: 22.6 us -> 6.02 us
    pallas_call x0 -> x1, Pallas kernels: none -> 117 us  [forward(): pl.pallas_call(functools.partial(forward_kernel, n_dp, n_mp, capacity), o...]
    all_gather x3 -> x0, waiting for transfers between devices: 97 us -> none  [the longest x1 71.9 us: per_device(): gathered = lax.all_gather(got_rows, 'mp', axis=1, tiled=True)]
    dot_general x12 -> x3, matrix products: 79.4 us -> 27.9 us  [the longest x1 12.1 us: per_device(): lax.dot_general(grad_keys.reshape(-1, query_width), w_key, NT, preferred_...]
    all_to_all x1 -> x0, blocking collectives: 18.7 us -> none  [per_device(): lax.all_to_all(send_rows, 'dp', split_axis=0, concat_axis=0, tiled=True)]
    gather x4 -> x0, local copies, waits for them, and re-layouts: 18.1 us -> none  [the longest x1 8.79 us: per_device(): encoded = jnp.take(gathered, chosen, axis=0)]
    convert_element_type x3 -> x0, local copies, waits for them, and re-layouts: 10.8 us -> none  [the longest x1 5.42 us: per_device(): grad_values = jnp.einsum('chqk,cqhd->ckhd', weights_bf, grad_blocks, pref...]
    reshape x4 -> x0, local copies, waits for them, and re-layouts: 9.93 us -> none  [the longest x1 4.96 us: per_device(): value_rows = value_rows.reshape(spans, MAXN * neigh_len, heads_dev, DH)]
    convert_element_type x1 -> x0, other arithmetic: 9.39 us -> none  [per_device(): spread.astype(jnp.bfloat16)]
  transfers between devices with their start and end apart: 7 -> 3, of which waited for: 7 -> 3; matrix products, arithmetic and copies ran while one was open for 8% -> 3% of each run, Pallas kernels for 0% -> 0%
where the time goes in v1:
time: 284 us
  Pallas kernels  117 us (41%)
  waiting for transfers between devices  111 us (39%)
  matrix products  27.9 us (10%)
  between operations  14.1 us (5%)
  other arithmetic  6.02 us (2%)
  starting transfers between devices  3.73 us (1%)
  local copies, waits for them, and re-layouts  3.47 us (1%)
    pallas_call x1, Pallas kernels, forward(): pl.pallas_call(functools.partial(forward_kernel, n_dp, n_mp, capacity), o...  117 us
    reduce_scatter x1, waiting for transfers between devices, per_device(): lax.psum_scatter(grad_enc.astype(jnp.bfloat16), 'mp', scatter_dimension=0...  79.7 us
    reduce_scatter x1, waiting for transfers between devices, per_device(): lax.psum_scatter(out_part.astype(jnp.bfloat16), 'mp', scatter_dimension=1...  20.6 us
    dot_general x1, matrix products, per_device(): lax.dot_general(grad_keys.reshape(-1, query_width), w_key, NT, preferred_...  12.1 us
    all_to_all x1, waiting for transfers between devices, per_device(): lax.all_to_all(grad_rows.reshape(groups, capacity, rows_dev, enc_width),...  10.9 us
    dot_general x1, matrix products, per_device(): lax.dot_general(grad_values.reshape(-1, query_width), w_value, NT, prefer...  9.67 us
    dot_general x1, matrix products, per_device(): out_part = jnp.dot(attended, w_out, preferred_element_type=jnp.float32)  6.13 us
  transfers between devices with their start and end apart: 3, of which 3 were waited for; matrix products, arithmetic and copies ran while one was open for 3% of the time, Pallas kernels for 0%

profile of v1, /device:TPU:0, one launch (start us, length us, event | category | flops | bytes accessed | tf_op | source)
XLA Modules:
  0.0 283.5 jit_solution(5777753003716723754)
XLA Ops:
  7.2 0.0 copy-start
  7.2 0.0 copy-start.4
  7.2 0.0 reduce-scatter.5.cloned.1.call-start
  7.2 0.7 fusion.2
  8.0 0.2 convert_reduce_fusion
  8.2 0.7 broadcast_compare_fusion
  8.8 0.1 fusion
  8.9 0.1 select_reduce_fusion
  9.1 0.1 sub.11
  9.2 0.0 copy-done
  9.2 0.6 gather_fusion
  9.8 1.8 pad_maximum_fusion.xd_in
  11.7 1.2 select_select_fusion.1
  12.8 0.7 broadcast_in_dim.72.tags_in
  13.5 0.0 copy-done.4
  13.5 0.6 broadcast_in_dim.73.counts_in
  14.1 117.0 %gather_attend.1 = (bf16[128,512]{1,0:T(8,128)(2,1)}, bf16[8,320,512]{2,1,0:T(8,128)(2,1)}, bf16[8,320,512]{2,1,0:T(8,128)(2,1)}) custom-call(bf16[256,1024]{1,0:T(8,128)(2,1)} %pad_maximum_fusion.xd_in, bf16[4,80,1536]{2,1,0:T(8,128)(2,1)} %bitcast.11, s32[4,8,128]{2,1,0:T(8,128)} %broadcast_in_dim.72.tags_in, s32[2,128]{1,0:T(2,128)} %broadcast_in_dim.73.counts_in, ...), custom_call_target="tpu_custom_call" | custom-call | tf_op jit(solution)/shard_map/gather_attend/pallas_call | solution.py:342
  131.2 0.0 copy-start.1
  131.2 12.1 %fusion.3 = f32[2560,1536]{1,0:T(8,128)} fusion(bf16[2560,512]{1,0:T(8,128)(2,1)} %bitcast.15, bf16[1536,512]{1,0:T(8,128)(2,1)} %wk_in.1), kind=kOutput, calls=%fused_computation.26 | convolution fusion | flops 4026531840 | bytes 19922944 | tf_op jit(solution)/shard_map/dot_general | solution.py:422
  143.3 0.0 copy-done.1
  143.3 9.7 %add_convert_fusion = bf16[2560,1536]{1,0:T(8,128)(2,1)} fusion(f32[2560,1536]{1,0:T(8,128)} %fusion.3, bf16[2560,512]{1,0:T(8,128)(2,1)S(1)} %bitcast.14, bf16[1536,512]{1,0:T(8,128)(2,1)S(1)} %copy-done.1), kind=kOutput, calls=%fused_computation.2 | convolution fusion | flops 4034396160 | bytes 27787264 | tf_op jit(solution)/shard_map/dot_general | solution.py:425
  153.0 0.0 reduce-scatter.5.cloned.1.call-update
  153.0 0.0 reduce-scatter.3.cloned.1.call-start
  153.1 0.8 copy-done.2
  153.9 6.1 %convolution_convert_fusion = bf16[128,8192]{1,0:T(8,128)(2,1)} fusion(bf16[128,512]{1,0:T(8,128)(2,1)S(1)} %copy-done.2, bf16[512,8192]{1,0:T(8,128)(2,1)} %wo_in.1), kind=kOutput, calls=%fused_computation.3 | convolution fusion | flops 1074790400 | bytes 10616832 | tf_op jit(solution)/shard_map/dot_general | solution.py:428
  160.0 0.0 reduce-scatter.3.cloned.1.call-update
  160.1 79.7 %reduce-scatter.5.cloned.1.call-done = bf16[320,1536]{1,0:T(8,128)(2,1)} async-done(((bf16[2560,1536]{1,0:T(8,128)(2,1)}), bf16[320,1536]{1,0:T(8,128)(2,1)}) %reduce-scatter.5.cloned.1.call-update) | async-done | bytes 983056 | tf_op jit(solution)/shard_map/reduce_scatter | solution.py:429
  239.8 3.7 %all-to-all-start = ((bf16[4,5,16,1536]{3,2,1,0:T(8,128)(2,1)}), bf16[4,5,16,1536]{3,2,1,0:T(8,128)(2,1)S(1)}, u32[]{:S(2)}, u32[]{:S(2)}) async-start(bf16[4,5,16,1536]{3,2,1,0:T(8,128)(2,1)} %bitcast.13), calls=%async_computation.2 | async-start | bytes 1966080 | tf_op jit(solution)/shard_map/all_to_all | solution.py:435
  243.4 10.9 %all-to-all-done = bf16[4,5,16,1536]{3,2,1,0:T(8,128)(2,1)S(1)} async-done(((bf16[4,5,16,1536]{3,2,1,0:T(8,128)(2,1)}), bf16[4,5,16,1536]{3,2,1,0:T(8,128)(2,1)S(1)}, u32[]{:S(2)}, u32[]{:S(2)}) %all-to-all-start) | async-done | bytes 983072 | tf_op jit(solution)/shard_map/all_to_all | solution.py:435
  254.3 0.6 gather_fusion.1
  254.9 1.2 select_select_fusion
  256.1 20.6 %reduce-scatter.3.cloned.1.call-done = bf16[128,1024]{1,0:T(8,128)(2,1)} async-done(((bf16[128,8192]{1,0:T(8,128)(2,1)}), bf16[128,1024]{1,0:T(8,128)(2,1)}) %reduce-scatter.3.cloned.1.call-update) | async-done | bytes 262160 | tf_op jit(solution)/shard_map/reduce_scatter | solution.py:432
  (9 shorter events, 0.0 us)
Async XLA Ops:
  7.2 2.0 copy-start
  7.2 6.3 %copy-start.4 = (s32[2]{0:T(128)S(1)}, s32[2]{0:T(128)}, u32[]{:S(2)}) copy-start(s32[2]{0:T(128)} %param.14) | copy-start | bytes 28
  7.2 232.6 %reduce-scatter.5.cloned.1.call-start = ((), (), s32[]{:S(2)}) async-start(), calls=%async_computation.4 | async-start | bytes 8847360 | tf_op jit(solution)/shard_map/reduce_scatter | solution.py:429
  131.2 12.2 %copy-start.1 = (bf16[1536,512]{1,0:T(8,128)(2,1)S(1)}, bf16[1536,512]{1,0:T(8,128)(2,1)}, u32[]{:S(2)}) copy-start(bf16[1536,512]{1,0:T(8,128)(2,1)} %wv_in.1) | copy-start | bytes 4718596
  131.2 12.1 %copy-start.3 = (bf16[8,320,512]{2,1,0:T(8,128)(2,1)S(1)}, bf16[8,320,512]{2,1,0:T(8,128)(2,1)}, u32[]{:S(2)}) copy-start(bf16[8,320,512]{2,1,0:T(8,128)(2,1)} %get-tuple-element.8) | copy-start | bytes 7864324
  153.0 0.9 copy-start.2
  153.0 123.7 %reduce-scatter.3.cloned.1.call-start = ((), (), s32[]{:S(2)}) async-start(), calls=%async_computation.3 | async-start | bytes 2359296 | tf_op jit(solution)/shard_map/reduce_scatter | solution.py:432
  239.8 14.6 %all-to-all-start = ((bf16[4,5,16,1536]{3,2,1,0:T(8,128)(2,1)}), bf16[4,5,16,1536]{3,2,1,0:T(8,128)(2,1)S(1)}, u32[]{:S(2)}, u32[]{:S(2)}) async-start(bf16[4,5,16,1536]{3,2,1,0:T(8,128)(2,1)} %bitcast.13), calls=%async_computation.2 | async-start | bytes 1966080 | tf_op jit(solution)/shard_map/all_to_all | solution.py:435
Sparse Core Ops, SparseCore 0:
  153.1 86.5 reduce-scatter.4
  242.6 33.9 reduce-scatter.2

commit v2 on v1

--- a/solution.py
+++ b/solution.py
@@ -379,6 +379,359 @@
     )(xd_shard, send_rows, send_tags, counts_rows, w_query, w_key, w_value, w_out)
 
 
+def backward_kernel(
+    n_dp,
+    n_mp,
+    att,
+    gk,
+    gv,
+    wk_in,
+    wv_in,
+    wo_in,
+    layer_out,
+    returned,
+    wk,
+    wv,
+    wo,
+    mine,
+    theirs,
+    paired,
+    landed,
+    out_mine,
+    out_theirs,
+    out_paired,
+    out_landed,
+    w_sem,
+    pair_send,
+    pair_recv,
+    out_pair_send,
+    out_pair_recv,
+    hop_send,
+    hop_recv,
+    out_send,
+    out_recv,
+    a2a_send,
+    a2a_recv,
+    own_sem,
+):
+    dp = lax.axis_index("dp")
+    mp = lax.axis_index("mp")
+    n_z = n_mp // 2
+    z = mp // 2
+    core = mp % 2
+    partner = {"mp": mp + 1 - 2 * core}
+    up = {"mp": lax.rem(mp + 2, n_mp)}
+    down = {"mp": lax.rem(mp + n_mp - 2, n_mp)}
+    has_up = z < n_z - 1
+    has_down = z > 0
+    chunk = mine.shape[1] // n_dp
+    feat = out_mine.shape[2]
+    bf = jnp.bfloat16
+
+    weight_copies = [
+        pltpu.make_async_copy(src, dst, w_sem.at[i])
+        for i, (src, dst) in enumerate(((wk_in, wk), (wv_in, wv), (wo_in, wo)))
+    ]
+    for copy in weight_copies:
+        copy.start()
+    greet(
+        [(None, {"dp": lax.rem(dp + k, n_dp)}) for k in range(1, n_dp)]
+        + [(None, partner), (has_up, up), (has_down, down)]
+    )
+    for copy in weight_copies:
+        copy.wait()
+
+    def pair_copy(d):
+        return pltpu.make_async_remote_copy(
+            src_ref=theirs.at[d],
+            dst_ref=paired.at[d],
+            send_sem=pair_send.at[d],
+            recv_sem=pair_recv.at[d],
+            device_id=partner,
+            device_id_type=MESH,
+        )
+
+    def out_pair_copy(d):
+        return pltpu.make_async_remote_copy(
+            src_ref=out_theirs.at[d],
+            dst_ref=out_paired.at[d],
+            send_sem=out_pair_send.at[d],
+            recv_sem=out_pair_recv.at[d],
+            device_id=partner,
+            device_id_type=MESH,
+        )
+
+    def grad_part(m):
+        return (dot_f32(gk[m], wk[...], NT) + dot_f32(gv[m], wv[...], NT)).astype(bf)
+
+    def out_part(m):
+        cols = pl.ds(pl.multiple_of(m * feat, feat), feat)
+        return dot_f32(att[...], wo[:, cols]).astype(bf)
+
+    def add(a, b):
+        return (a.astype(jnp.float32) + b.astype(jnp.float32)).astype(bf)
+
+    def prepare(d):
+        own, other = d * 2 + core, d * 2 + 1 - core
+        theirs[d] = grad_part(other)
+        pair_copy(d).start()
+        out_theirs[d] = out_part(other)
+        out_pair_copy(d).start()
+        mine[d] = grad_part(own)
+        out_mine[d] = out_part(own)
+        pair_copy(d).wait()
+        mine[d] = add(mine[d], paired[d])
+        out_pair_copy(d).wait()
+        out_mine[d] = add(out_mine[d], out_paired[d])
+
+    def target(direction, k):
+        j = k // n_dp
+        return n_z - 1 - j if direction == 0 else j
+
+    def slot_of(direction, d):
+        return d if direction == 0 else jnp.where(d == z - 1, n_z, d)
+
+    def hop(direction, k):
+        d = target(direction, k)
+        rows = pl.ds(pl.multiple_of((k % n_dp) * chunk, chunk), chunk)
+        slot = slot_of(direction, d)
+        return pltpu.make_async_remote_copy(
+            src_ref=mine.at[d, rows],
+            dst_ref=landed.at[slot, rows],
+            send_sem=hop_send.at[direction, k],
+            recv_sem=hop_recv.at[slot, k % n_dp],
+            device_id=(up, down)[direction],
+            device_id_type=MESH,
+        )
+
+    def hop_arrived(slot, g):
+        rows = pl.ds(pl.multiple_of(g * chunk, chunk), chunk)
+        pltpu.make_async_remote_copy(
+            src_ref=landed.at[slot, rows],
+            dst_ref=landed.at[slot, rows],
+            send_sem=hop_send.at[0, 0],
+            recv_sem=hop_recv.at[slot, g],
+            device_id=partner,
+            device_id_type=MESH,
+        ).wait_recv()
+        return rows
+
+    def out_hop(direction, j):
+        d = n_z - 1 - j if direction == 0 else j
+        slot = slot_of(direction, d)
+        return pltpu.make_async_remote_copy(
+            src_ref=out_mine.at[d],
+            dst_ref=out_landed.at[slot],
+            send_sem=out_send.at[direction, j],
+            recv_sem=out_recv.at[slot],
+            device_id=(up, down)[direction],
+            device_id_type=MESH,
+        )
+
+    def out_arrived(slot):
+        pltpu.make_async_remote_copy(
+            src_ref=out_landed.at[slot],
+            dst_ref=out_landed.at[slot],
+            send_sem=out_send.at[0, 0],
+            recv_sem=out_recv.at[slot],
+            device_id=partner,
+            device_id_type=MESH,
+        ).wait_recv()
+
+    sent = (n_z - 1 - z, z)
+    from_behind = (has_down, has_up)
+
+    def step(s, carry):
+        items = []
+        for direction in range(2):
+            j = s - (z if direction == 0 else n_z - 1 - z)
+            d = n_z - 1 - j if direction == 0 else j
+            active = jnp.logical_and(j >= 0, j < sent[direction])
+            items.append((direction, j, d, active))
+
+            @pl.when(active)
+            def _(d=d):
+                prepare(d)
+
+        for direction, j, d, active in items:
+
+            @pl.when(active)
+            def _(direction=direction, j=j, d=d):
+                @pl.when(from_behind[direction])
+                def _():
+                    out_arrived(d)
+                    out_mine[d] = add(out_mine[d], out_landed[d])
+
+                out_hop(direction, j).start()
+
+        def each(g, c):
+            for direction, j, d, active in items:
+
+                @pl.when(active)
+                def _(direction=direction, j=j, d=d):
+                    @pl.when(from_behind[direction])
+                    def _():
+                        rows = hop_arrived(d, g)
+                        mine[d, rows, :] = add(mine[d, rows, :], landed[d, rows, :])
+
+                    k = j * n_dp + g
+
+                    @pl.when(k >= 2)
+                    def _():
+                        hop(direction, k - 2).wait_send()
+
+                    hop(direction, k).start()
+
+            return c
+
+        lax.fori_loop(0, n_dp, each, 0)
+        return carry
+
+    lax.fori_loop(0, n_z - 1, step, 0)
+
+    prepare(z)
+
+    @pl.when(has_down)
+    def _():
+        out_arrived(z)
+        out_mine[z] = add(out_mine[z], out_landed[z])
+
+    @pl.when(has_up)
+    def _():
+        out_arrived(n_z)
+        out_mine[z] = add(out_mine[z], out_landed[n_z])
+
+    layer_out[...] = out_mine[z]
+
+    def back(g):
+        rows = pl.ds(pl.multiple_of(g * chunk, chunk), chunk)
+        return pltpu.make_async_remote_copy(
+            src_ref=mine.at[z, rows],
+            dst_ref=returned.at[dp],
+            send_sem=a2a_send.at[g],
+            recv_sem=a2a_recv.at[dp],
+            device_id={"dp": g},
+            device_id_type=MESH,
+        )
+
+    def back_arrived(g):
+        rows = pl.ds(pl.multiple_of(g * chunk, chunk), chunk)
+        pltpu.make_async_remote_copy(
+            src_ref=mine.at[z, rows],
+            dst_ref=returned.at[g],
+            send_sem=a2a_send.at[g],
+            recv_sem=a2a_recv.at[g],
+            device_id={"dp": g},
+            device_id_type=MESH,
+        ).wait_recv()
+
+    own_rows = pl.ds(pl.multiple_of(dp * chunk, chunk), chunk)
+    own_copy = pltpu.make_async_copy(mine.at[z, own_rows], returned.at[dp], own_sem)
+
+    def last(g, c):
+        rows = pl.ds(pl.multiple_of(g * chunk, chunk), chunk)
+
+        @pl.when(has_down)
+        def _():
+            hop_arrived(z, g)
+            mine[z, rows, :] = add(mine[z, rows, :], landed[z, rows, :])
+
+        @pl.when(has_up)
+        def _():
+            hop_arrived(n_z, g)
+            mine[z, rows, :] = add(mine[z, rows, :], landed[n_z, rows, :])
+
+        @pl.when(g != dp)
+        def _():
+            back(g).start()
+
+        @pl.when(g == dp)
+        def _():
+            own_copy.start()
+
+        return c
+
+    lax.fori_loop(0, n_dp, last, 0)
+    own_copy.wait()
+
+    def finish(g, c):
+        @pl.when(g != dp)
+        def _():
+            back(g).wait_send()
+            back_arrived(g)
+
+        return c
+
+    lax.fori_loop(0, n_dp, finish, 0)
+
+    for direction in range(2):
+
+        @pl.when(sent[direction] > 0)
+        def _(direction=direction):
+            count = sent[direction] * n_dp
+            hop(direction, count - 2).wait_send()
+            hop(direction, count - 1).wait_send()
+
+        def drain(j, c, direction=direction):
+            @pl.when(j < sent[direction])
+            def _():
+                out_hop(direction, j).wait_send()
+
+            return c
+
+        lax.fori_loop(0, n_z - 1, drain, 0)
+
+
+def backward(att, gk, gv, w_key, w_value, w_out, n_dp, n_mp):
+    tokens = att.shape[0]
+    shard = gk.shape[1]
+    enc = w_key.shape[0]
+    feat = w_out.shape[1] // n_mp
+    n_z = n_mp // 2
+    bf = jnp.bfloat16
+    hbm = pl.BlockSpec(memory_space=pl.ANY)
+    vm = pl.BlockSpec(memory_space=pltpu.VMEM)
+    dma = pltpu.SemaphoreType.DMA
+    return pl.pallas_call(
+        functools.partial(backward_kernel, n_dp, n_mp),
+        out_shape=(
+            jax.ShapeDtypeStruct((tokens, feat), bf),
+            jax.ShapeDtypeStruct((n_dp, shard // n_dp, enc), bf),
+        ),
+        in_specs=[vm, vm, vm, hbm, hbm, hbm],
+        out_specs=(vm, hbm),
+        scratch_shapes=[
+            pltpu.VMEM(w_key.shape, bf),
+            pltpu.VMEM(w_value.shape, bf),
+            pltpu.VMEM(w_out.shape, bf),
+            pltpu.VMEM((n_z, shard, enc), bf),
+            pltpu.VMEM((n_z, shard, enc), bf),
+            pltpu.VMEM((n_z, shard, enc), bf),
+            pltpu.VMEM((n_z + 1, shard, enc), bf),
+            pltpu.VMEM((n_z, tokens, feat), bf),
+            pltpu.VMEM((n_z, tokens, feat), bf),
+            pltpu.VMEM((n_z, tokens, feat), bf),
+            pltpu.VMEM((n_z + 1, tokens, feat), bf),
+            dma((3,)),
+            dma((n_z,)),
+            dma((n_z,)),
+            dma((n_z,)),
+            dma((n_z,)),
+            dma((2, n_z * n_dp)),
+            dma((n_z + 1, n_dp)),
+            dma((2, n_z)),
+            dma((n_z + 1,)),
+            dma((n_dp,)),
+            dma((n_dp,)),
+            dma,
+        ],
+        compiler_params=pltpu.CompilerParams(
+            collective_id=1, has_side_effects=True, vmem_limit_bytes=VMEM_LIMIT
+        ),
+        name="grads_scatter",
+    )(att, gk, gv, w_key, w_value, w_out)
+
+
 def per_device(hidden_in, out_grad, neighbours, counts, slot_owner, w_query, w_key, w_value, w_out):
     groups = lax.axis_size("dp")
     n_mp = lax.axis_size("mp")
@@ -388,7 +741,6 @@
     capacity = src_slots // groups
     rows_dev = neighbours.shape[1]
     enc_width = neighbours.shape[2]
-    query_width = w_query.shape[1]
     slot_order = jnp.arange(src_slots, dtype=jnp.int32)
     dest_group = jnp.where(slot_owner >= 0, slot_owner // slots_group, -1)
     earlier = (dest_group[None, :] == dest_group[:, None]) & (
@@ -419,25 +771,8 @@
         groups,
         n_mp,
     )
-    grad_enc = lax.dot_general(
-        grad_keys.reshape(-1, query_width), w_key, NT, preferred_element_type=jnp.float32
-    )
-    grad_enc = grad_enc + lax.dot_general(
-        grad_values.reshape(-1, query_width), w_value, NT, preferred_element_type=jnp.float32
-    )
-    out_part = jnp.dot(attended, w_out, preferred_element_type=jnp.float32)
-    grad_rows = lax.psum_scatter(
-        grad_enc.astype(jnp.bfloat16), "mp", scatter_dimension=0, tiled=True
-    )
-    layer_out = lax.psum_scatter(
-        out_part.astype(jnp.bfloat16), "mp", scatter_dimension=1, tiled=True
-    )
-    returned = lax.all_to_all(
-        grad_rows.reshape(groups, capacity, rows_dev, enc_width),
-        "dp",
-        split_axis=0,
-        concat_axis=0,
-        tiled=True,
+    layer_out, returned = backward(
+        attended, grad_keys, grad_values, w_key, w_value, w_out, groups, n_mp
     )
     returned = returned.reshape(src_slots, rows_dev, enc_width)
     neighbour_grad = jnp.where(

time: 284 us -> 234 us (0.82)
  the two profiles are of different devices: /device:TPU:0 before, /device:TPU:15 now
where the time goes in v2:
time: 234 us
  Pallas kernels  223 us (95%)
  other arithmetic  5.05 us (2%)
  local copies, waits for them, and re-layouts  4.62 us (2%)
    pallas_call x1, Pallas kernels, backward(): pl.pallas_call(functools.partial(backward_kernel, n_dp, n_mp), out_shape=...  123 us
    pallas_call x1, Pallas kernels, forward(): pl.pallas_call(functools.partial(forward_kernel, n_dp, n_mp, capacity), o...  101 us

profile of v2, /device:TPU:15, one launch (start us, length us, event | category | flops | bytes accessed | tf_op | source)
XLA Modules:
  0.0 233.9 jit_solution(5727047217380983408)
XLA Ops:
  0.6 0.0 copy-start
  0.6 0.0 copy-start.3
  0.7 0.0 copy-start.2
  0.7 0.0 copy-start.4
  0.7 0.8 fusion.2
  1.5 0.2 convert_reduce_fusion
  1.6 0.7 broadcast_compare_fusion
  2.3 0.1 select_reduce_fusion
  2.4 0.0 copy-done
  2.4 0.6 gather_fusion
  3.1 0.1 fusion
  3.2 1.2 select_select_fusion.1
  4.4 0.1 sub.11
  4.5 0.7 broadcast_in_dim.72.tags_in
  5.1 0.0 copy-done.3
  5.1 0.0 copy-done.2
  5.1 0.8 pad_maximum_fusion.xd_in
  6.0 0.0 copy-done.4
  6.0 0.7 broadcast_in_dim.73.counts_in
  6.6 100.7 %gather_attend.1 = (bf16[128,512]{1,0:T(8,128)(2,1)}, bf16[8,320,512]{2,1,0:T(8,128)(2,1)}, bf16[8,320,512]{2,1,0:T(8,128)(2,1)}) custom-call(bf16[256,1024]{1,0:T(8,128)(2,1)} %pad_maximum_fusion.xd_in, bf16[4,80,1536]{2,1,0:T(8,128)(2,1)} %bitcast.2, s32[4,8,128]{2,1,0:T(8,128)} %broadcast_in_dim.72.tags_in, s32[2,128]{1,0:T(2,128)} %broadcast_in_dim.73.counts_in, ...), custom_call_target="tpu_custom_call" | custom-call | tf_op jit(solution)/shard_map/gather_attend/pallas_call | solution.py:342
  107.4 122.7 %grads_scatter.1 = (bf16[128,1024]{1,0:T(8,128)(2,1)}, bf16[4,80,1536]{2,1,0:T(8,128)(2,1)}) custom-call(bf16[128,512]{1,0:T(8,128)(2,1)} %get-tuple-element.8.att, bf16[8,320,512]{2,1,0:T(8,128)(2,1)} %get-tuple-element.9.gk, bf16[8,320,512]{2,1,0:T(8,128)(2,1)} %get-tuple-element.10.gv, bf16[1536,512]{1,0:T(8,128)(2,1)} %wk_in.3, bf16[1536,512]{1,0:T(8,128)(2,1)} %wv_in.3, ...), custom_call_target="tpu_custom_call" | custom-call | tf_op jit(solution)/shard_map/grads_scatter/pallas_call | solution.py:695
  230.1 0.0 copy-start.1
  230.1 1.8 gather_fusion.1
  232.0 1.2 select_select_fusion
  233.1 0.0 copy-done.1
  233.1 0.7 copy.12
  (6 shorter events, 0.0 us)
Async XLA Ops:
  0.6 1.8 copy-start
  0.6 4.5 %copy-start.3 = (bf16[128,1024]{1,0:T(8,128)(2,1)S(1)}, bf16[128,1024]{1,0:T(8,128)(2,1)}, u32[]{:S(2)}) copy-start(bf16[128,1024]{1,0:T(8,128)(2,1)} %param.11) | copy-start | bytes 786436
  0.7 4.5 %copy-start.2 = (bf16[128,1024]{1,0:T(8,128)(2,1)S(1)}, bf16[128,1024]{1,0:T(8,128)(2,1)}, u32[]{:S(2)}) copy-start(bf16[128,1024]{1,0:T(8,128)(2,1)} %param.12) | copy-start | bytes 786436
  0.7 5.3 %copy-start.4 = (s32[2]{0:T(128)S(1)}, s32[2]{0:T(128)}, u32[]{:S(2)}) copy-start(s32[2]{0:T(128)} %param.14) | copy-start | bytes 28
  230.1 3.1 %copy-start.1 = (bf16[128,1024]{1,0:T(8,128)(2,1)S(1)}, bf16[128,1024]{1,0:T(8,128)(2,1)}, u32[]{:S(2)}) copy-start(bf16[128,1024]{1,0:T(8,128)(2,1)} %get-tuple-element.24) | copy-start | bytes 786436

commit v3 on v2

--- a/solution.py
+++ b/solution.py
@@ -59,7 +59,8 @@
     wk,
     wv,
     wo,
-    keys,
+    scores,
+    grad_w,
     vals,
     queries,
     grads,
@@ -225,59 +226,6 @@
 
     lax.fori_loop(1, n_z, xd_step, 0)
 
-    def project(slot):
-        rows = nb[slot]
-        keys[slot] = dot_f32(rows, wk[...]).astype(jnp.bfloat16)
-        vals[slot] = dot_f32(rows, wv[...]).astype(jnp.bfloat16)
-
-    def both_cores(origin):
-        arrived(*nb_args, origin * 2 + 1 - core)
-
-        def step(c, carry):
-            project(origin * 2 + c)
-            return carry
-
-        lax.fori_loop(0, 2, step, 0)
-
-    def nb_step(s, carry):
-        relay(nb_args, s)
-
-        @pl.when(s == 1)
-        def _():
-            for copy in weight_copies:
-                copy.wait()
-
-            def other(origin, c):
-                arrived(*xd_args, origin * 2 + 1 - core)
-                return c
-
-            lax.fori_loop(0, n_z, other, 0)
-
-            def add(m, c):
-                q, g = c
-                cols = pl.ds(pl.multiple_of(m * feat, feat), feat)
-                q = q + dot_f32(xd[m, :tokens, :], wq[cols, :])
-                g = g + dot_f32(xd[m, tokens:, :], wo[:, cols], NT)
-                return (q, g)
-
-            zero = jnp.zeros(queries.shape, jnp.float32)
-            q, g = lax.fori_loop(0, n_mp, add, (zero, zero))
-            queries[...] = q.astype(jnp.bfloat16)
-            grads[...] = g.astype(jnp.bfloat16)
-            both_cores(z)
-
-        @pl.when(z - s >= 0)
-        def _():
-            both_cores(z - s)
-
-        @pl.when(z + s <= n_z - 1)
-        def _():
-            both_cores(z + s)
-
-        return carry
-
-    lax.fori_loop(1, n_z, nb_step, 0)
-
     span_len = tokens // (counts_in.shape[0])
     lane = lax.broadcasted_iota(jnp.int32, (1, tokens), 1)
     spans = counts_in.shape[0]
@@ -298,25 +246,82 @@
             bias[low : low + width, :] = jnp.broadcast_to(value, (width, tokens))
 
     scale = 1.0 / math.sqrt(DH)
+
+    def project(slot):
+        rows = nb[slot]
+        k_rows = dot_f32(rows, wk[...]).astype(jnp.bfloat16)
+        v_rows = dot_f32(rows, wv[...]).astype(jnp.bfloat16)
+        vals[slot] = v_rows
+        for h in range(queries.shape[1] // DH):
+            cols = slice(h * DH, (h + 1) * DH)
+            scores[h, slot] = dot_f32(k_rows[:, cols], queries[:, cols], NT) * scale + bias[...]
+            grad_w[h, slot] = dot_f32(v_rows[:, cols], grads[:, cols], NT)
+
+    def both_cores(origin):
+        arrived(*nb_args, origin * 2 + 1 - core)
+
+        def step(c, carry):
+            project(origin * 2 + c)
+            return carry
+
+        lax.fori_loop(0, 2, step, 0)
+
+    def nb_step(s, carry):
+        relay(nb_args, s)
+
+        @pl.when(s == 1)
+        def _():
+            for copy in weight_copies:
+                copy.wait()
+
+            def other(origin, c):
+                arrived(*xd_args, origin * 2 + 1 - core)
+                return c
+
+            lax.fori_loop(0, n_z, other, 0)
+
+            def add(m, c):
+                q, g = c
+                cols = pl.ds(pl.multiple_of(m * feat, feat), feat)
+                q = q + dot_f32(xd[m, :tokens, :], wq[cols, :])
+                g = g + dot_f32(xd[m, tokens:, :], wo[:, cols], NT)
+                return (q, g)
+
+            zero = jnp.zeros(queries.shape, jnp.float32)
+            q, g = lax.fori_loop(0, n_mp, add, (zero, zero))
+            queries[...] = q.astype(jnp.bfloat16)
+            grads[...] = g.astype(jnp.bfloat16)
+            both_cores(z)
+
+        @pl.when(z - s >= 0)
+        def _():
+            both_cores(z - s)
+
+        @pl.when(z + s <= n_z - 1)
+        def _():
+            both_cores(z + s)
+
+        return carry
+
+    lax.fori_loop(1, n_z, nb_step, 0)
+
     shard = nb.shape[1]
     total = n_mp * shard
     for h in range(queries.shape[1] // DH):
         cols = slice(h * DH, (h + 1) * DH)
         q = queries[:, cols]
         g = grads[:, cols]
-        k = keys[:, :, cols].reshape(total, DH)
         v = vals[:, :, cols].reshape(total, DH)
-        scores = dot_f32(k, q, NT) * scale
-        scores = (scores.reshape(n_mp, shard, tokens) + bias[...][None]).reshape(total, tokens)
-        peak = jnp.max(scores, axis=0, keepdims=True)
-        expo = jnp.exp(scores - peak)
+        score = scores[h].reshape(total, tokens)
+        peak = jnp.max(score, axis=0, keepdims=True)
+        expo = jnp.exp(score - peak)
         weights = expo * (1.0 / jnp.sum(expo, axis=0, keepdims=True))
         weights_bf = weights.astype(jnp.bfloat16)
         att_out[:, cols] = dot_f32(weights_bf, v, TN).astype(jnp.bfloat16)
         gv_out[:, :, cols] = dot_f32(weights_bf, g).astype(jnp.bfloat16).reshape(n_mp, shard, DH)
-        grad_w = dot_f32(v, g, NT)
-        inner = jnp.sum(weights * grad_w, axis=0, keepdims=True)
-        grad_s = (weights * (grad_w - inner) * scale).astype(jnp.bfloat16)
+        grad_h = grad_w[h].reshape(total, tokens)
+        inner = jnp.sum(weights * grad_h, axis=0, keepdims=True)
+        grad_s = (weights * (grad_h - inner) * scale).astype(jnp.bfloat16)
         gk_out[:, :, cols] = dot_f32(grad_s, q).astype(jnp.bfloat16).reshape(n_mp, shard, DH)
 
     drain(xd_args)
@@ -356,7 +361,8 @@
             pltpu.VMEM(w_key.shape, bf),
             pltpu.VMEM(w_value.shape, bf),
             pltpu.VMEM(w_out.shape, bf),
-            pltpu.VMEM((n_mp, shard, width), bf),
+            pltpu.VMEM((width // DH, n_mp, shard, tokens), jnp.float32),
+            pltpu.VMEM((width // DH, n_mp, shard, tokens), jnp.float32),
             pltpu.VMEM((n_mp, shard, width), bf),
             pltpu.VMEM((tokens, width), bf),
             pltpu.VMEM((tokens, width), bf),
@@ -471,7 +477,7 @@
     def add(a, b):
         return (a.astype(jnp.float32) + b.astype(jnp.float32)).astype(bf)
 
-    def prepare(d):
+    def start_parts(d):
         own, other = d * 2 + core, d * 2 + 1 - core
         theirs[d] = grad_part(other)
         pair_copy(d).start()
@@ -479,10 +485,12 @@
         out_pair_copy(d).start()
         mine[d] = grad_part(own)
         out_mine[d] = out_part(own)
+
+    def finish_parts(d):
+        out_pair_copy(d).wait()
+        out_mine[d] = add(out_mine[d], out_paired[d])
         pair_copy(d).wait()
         mine[d] = add(mine[d], paired[d])
-        out_pair_copy(d).wait()
-        out_mine[d] = add(out_mine[d], out_paired[d])
 
     def target(direction, k):
         j = k // n_dp
@@ -541,17 +549,26 @@
     sent = (n_z - 1 - z, z)
     from_behind = (has_down, has_up)
 
-    def step(s, carry):
+    def at_step(s):
         items = []
         for direction in range(2):
             j = s - (z if direction == 0 else n_z - 1 - z)
             d = n_z - 1 - j if direction == 0 else j
-            active = jnp.logical_and(j >= 0, j < sent[direction])
-            items.append((direction, j, d, active))
+            items.append((direction, j, d, jnp.logical_and(j >= 0, j < sent[direction])))
+        return items
+
+    @pl.when(jnp.logical_or(z == 0, z == n_z - 1))
+    def _():
+        start_parts(n_z - 1 - z)
+
+    def step(s, carry):
+        items = at_step(s)
+        following = at_step(s + 1)
+        for direction, j, d, active in items:
 
             @pl.when(active)
             def _(d=d):
-                prepare(d)
+                finish_parts(d)
 
         for direction, j, d, active in items:
 
@@ -582,6 +599,17 @@
 
                     hop(direction, k).start()
 
+            wanted = jnp.logical_and(g == 2, s == n_z - 2)
+            part = z
+            for direction, j, d, active in following:
+                here = g == direction
+                wanted = jnp.logical_or(wanted, jnp.logical_and(here, active))
+                part = jnp.where(here, d, part)
+
+            @pl.when(wanted)
+            def _():
+                start_parts(part)
+
             return c
 
         lax.fori_loop(0, n_dp, each, 0)
@@ -589,7 +617,7 @@
 
     lax.fori_loop(0, n_z - 1, step, 0)
 
-    prepare(z)
+    finish_parts(z)
 
     @pl.when(has_down)
     def _():

time: 234 us -> 232 us (level)
  no operation moved by 1% of the time
where the time goes in v3:
time: 232 us
  Pallas kernels  222 us (96%)
  other arithmetic  5.05 us (2%)
  local copies, waits for them, and re-layouts  4.62 us (2%)
    pallas_call x1, Pallas kernels, backward(): pl.pallas_call(functools.partial(backward_kernel, n_dp, n_mp), out_shape=...  121 us
    pallas_call x1, Pallas kernels, forward(): pl.pallas_call(functools.partial(forward_kernel, n_dp, n_mp, capacity), o...  101 us

profile of v3, /device:TPU:15, one launch (start us, length us, event | category | flops | bytes accessed | tf_op | source)
XLA Modules:
  0.0 232.1 jit_solution(10794578243809328162)
XLA Ops:
  0.6 0.0 copy-start
  0.6 0.0 copy-start.3
  0.7 0.0 copy-start.2
  0.7 0.0 copy-start.4
  0.7 0.8 fusion.2
  1.5 0.2 convert_reduce_fusion
  1.6 0.7 broadcast_compare_fusion
  2.3 0.1 select_reduce_fusion
  2.4 0.0 copy-done
  2.4 0.6 gather_fusion
  3.1 0.1 fusion
  3.2 1.2 select_select_fusion.1
  4.4 0.1 sub.11
  4.5 0.7 broadcast_in_dim.72.tags_in
  5.1 0.0 copy-done.3
  5.1 0.0 copy-done.2
  5.1 0.8 pad_maximum_fusion.xd_in
  6.0 0.0 copy-done.4
  6.0 0.7 broadcast_in_dim.73.counts_in
  6.6 100.8 %gather_attend.1 = (bf16[128,512]{1,0:T(8,128)(2,1)}, bf16[8,320,512]{2,1,0:T(8,128)(2,1)}, bf16[8,320,512]{2,1,0:T(8,128)(2,1)}) custom-call(bf16[256,1024]{1,0:T(8,128)(2,1)} %pad_maximum_fusion.xd_in, bf16[4,80,1536]{2,1,0:T(8,128)(2,1)} %bitcast.2, s32[4,8,128]{2,1,0:T(8,128)} %broadcast_in_dim.72.tags_in, s32[2,128]{1,0:T(2,128)} %broadcast_in_dim.73.counts_in, ...), custom_call_target="tpu_custom_call" | custom-call | tf_op jit(solution)/shard_map/gather_attend/pallas_call | solution.py:347
  107.4 120.9 %grads_scatter.1 = (bf16[128,1024]{1,0:T(8,128)(2,1)}, bf16[4,80,1536]{2,1,0:T(8,128)(2,1)}) custom-call(bf16[128,512]{1,0:T(8,128)(2,1)} %get-tuple-element.8.att, bf16[8,320,512]{2,1,0:T(8,128)(2,1)} %get-tuple-element.9.gk, bf16[8,320,512]{2,1,0:T(8,128)(2,1)} %get-tuple-element.10.gv, bf16[1536,512]{1,0:T(8,128)(2,1)} %wk_in.3, bf16[1536,512]{1,0:T(8,128)(2,1)} %wv_in.3, ...), custom_call_target="tpu_custom_call" | custom-call | tf_op jit(solution)/shard_map/grads_scatter/pallas_call | solution.py:723
  228.4 0.0 copy-start.1
  228.4 1.8 gather_fusion.1
  230.3 1.2 select_select_fusion
  231.4 0.0 copy-done.1
  231.4 0.7 copy.12
  (6 shorter events, 0.0 us)
Async XLA Ops:
  0.6 1.8 copy-start
  0.6 4.5 %copy-start.3 = (bf16[128,1024]{1,0:T(8,128)(2,1)S(1)}, bf16[128,1024]{1,0:T(8,128)(2,1)}, u32[]{:S(2)}) copy-start(bf16[128,1024]{1,0:T(8,128)(2,1)} %param.11) | copy-start | bytes 786436
  0.7 4.5 %copy-start.2 = (bf16[128,1024]{1,0:T(8,128)(2,1)S(1)}, bf16[128,1024]{1,0:T(8,128)(2,1)}, u32[]{:S(2)}) copy-start(bf16[128,1024]{1,0:T(8,128)(2,1)} %param.12) | copy-start | bytes 786436
  0.7 5.3 %copy-start.4 = (s32[2]{0:T(128)S(1)}, s32[2]{0:T(128)}, u32[]{:S(2)}) copy-start(s32[2]{0:T(128)} %param.14) | copy-start | bytes 28
  228.4 3.1 %copy-start.1 = (bf16[128,1024]{1,0:T(8,128)(2,1)S(1)}, bf16[128,1024]{1,0:T(8,128)(2,1)}, u32[]{:S(2)}) copy-start(bf16[128,1024]{1,0:T(8,128)(2,1)} %get-tuple-element.24) | copy-start | bytes 786436

commit v4 on v3

--- a/solution.py
+++ b/solution.py
@@ -41,7 +41,8 @@
     n_dp,
     n_mp,
     capacity,
-    xd_in,
+    x_in,
+    dy_in,
     rows_in,
     tags_in,
     counts_in,
@@ -169,12 +170,14 @@
     xd_args = (xd, xd_send, xd_recv)
     nb_args = (nb, nb_send, nb_recv)
 
-    own_xd = pltpu.make_async_copy(xd_in, xd.at[mp], own_sem.at[0])
+    own_x = pltpu.make_async_copy(x_in, xd.at[mp, pl.ds(0, tokens)], own_sem.at[0])
+    own_dy = pltpu.make_async_copy(dy_in, xd.at[mp, pl.ds(tokens, tokens)], own_sem.at[3])
     own_rows = pltpu.make_async_copy(
         rows_in.at[dp], nb.at[mp, pl.ds(dp * block, block)], own_sem.at[1]
     )
     own_tags = pltpu.make_async_copy(tags_in.at[dp], tags.at[dp], own_sem.at[2])
-    own_xd.start()
+    own_x.start()
+    own_dy.start()
     own_rows.start()
     own_tags.start()
     greet(
@@ -208,7 +211,8 @@
         row_copy(k).start()
     for k in range(1, n_dp):
         tag_copy(k).start()
-    own_xd.wait()
+    own_x.wait()
+    own_dy.wait()
     send_own(xd_args)
     for copy in weight_copies:
         copy.start()
@@ -258,10 +262,14 @@
             grad_w[h, slot] = dot_f32(v_rows[:, cols], grads[:, cols], NT)
 
     def both_cores(origin):
-        arrived(*nb_args, origin * 2 + 1 - core)
-
-        def step(c, carry):
-            project(origin * 2 + c)
+        def step(i, carry):
+            slot = origin * 2 + jnp.where(i == 0, core, 1 - core)
+
+            @pl.when(i == 1)
+            def _():
+                arrived(*nb_args, slot)
+
+            project(slot)
             return carry
 
         lax.fori_loop(0, 2, step, 0)
@@ -328,9 +336,9 @@
     drain(nb_args)
 
 
-def forward(xd_shard, send_rows, send_tags, counts_rows, w_query, w_key, w_value, w_out, n_dp, n_mp):
+def forward(x_shard, dy_shard, send_rows, send_tags, counts_rows, w_query, w_key, w_value, w_out, n_dp, n_mp):
     capacity = send_tags.shape[1]
-    tokens = xd_shard.shape[0] // 2
+    tokens, feat = x_shard.shape
     send_tags = jnp.broadcast_to(
         jnp.pad(send_tags, ((0, 0), (0, -capacity % 8)), constant_values=-1)[:, :, None],
         (n_dp, capacity + (-capacity % 8), tokens),
@@ -351,10 +359,10 @@
             jax.ShapeDtypeStruct((n_mp, shard, width), bf),
             jax.ShapeDtypeStruct((n_mp, shard, width), bf),
         ),
-        in_specs=[hbm, hbm, hbm, vm, hbm, hbm, hbm, hbm],
+        in_specs=[hbm, hbm, hbm, hbm, vm, hbm, hbm, hbm, hbm],
         out_specs=(vm, vm, vm),
         scratch_shapes=[
-            pltpu.VMEM((n_mp,) + xd_shard.shape, bf),
+            pltpu.VMEM((n_mp, 2 * tokens, feat), bf),
             pltpu.VMEM((n_mp, shard, enc), bf),
             pltpu.VMEM(send_tags.shape, jnp.int32),
             pltpu.VMEM(w_query.shape, bf),
@@ -372,7 +380,7 @@
             dma((n_dp,)),
             dma((n_dp,)),
             dma((n_dp,)),
-            dma((3,)),
+            dma((4,)),
             dma((3, n_z)),
             dma((n_mp,)),
             dma((3, n_z)),
@@ -382,20 +390,22 @@
             collective_id=0, has_side_effects=True, vmem_limit_bytes=VMEM_LIMIT
         ),
         name="gather_attend",
-    )(xd_shard, send_rows, send_tags, counts_rows, w_query, w_key, w_value, w_out)
+    )(x_shard, dy_shard, send_rows, send_tags, counts_rows, w_query, w_key, w_value, w_out)
 
 
 def backward_kernel(
     n_dp,
     n_mp,
     att,
-    gk,
-    gv,
+    gk_in,
+    gv_in,
     wk_in,
     wv_in,
     wo_in,
     layer_out,
     returned,
+    gk,
+    gv,
     wk,
     wv,
     wo,
@@ -436,7 +446,9 @@
 
     weight_copies = [
         pltpu.make_async_copy(src, dst, w_sem.at[i])
-        for i, (src, dst) in enumerate(((wk_in, wk), (wv_in, wv), (wo_in, wo)))
+        for i, (src, dst) in enumerate(
+            ((wk_in, wk), (wv_in, wv), (gk_in, gk), (gv_in, gv), (wo_in, wo))
+        )
     ]
     for copy in weight_copies:
         copy.start()
@@ -444,7 +456,7 @@
         [(None, {"dp": lax.rem(dp + k, n_dp)}) for k in range(1, n_dp)]
         + [(None, partner), (has_up, up), (has_down, down)]
     )
-    for copy in weight_copies:
+    for copy in weight_copies[:-1]:
         copy.wait()
 
     def pair_copy(d):
@@ -477,14 +489,15 @@
     def add(a, b):
         return (a.astype(jnp.float32) + b.astype(jnp.float32)).astype(bf)
 
-    def start_parts(d):
-        own, other = d * 2 + core, d * 2 + 1 - core
-        theirs[d] = grad_part(other)
+    def start_grads(d):
+        theirs[d] = grad_part(d * 2 + 1 - core)
         pair_copy(d).start()
-        out_theirs[d] = out_part(other)
+        mine[d] = grad_part(d * 2 + core)
+
+    def start_out(d):
+        out_theirs[d] = out_part(d * 2 + 1 - core)
         out_pair_copy(d).start()
-        mine[d] = grad_part(own)
-        out_mine[d] = out_part(own)
+        out_mine[d] = out_part(d * 2 + core)
 
     def finish_parts(d):
         out_pair_copy(d).wait()
@@ -557,9 +570,17 @@
             items.append((direction, j, d, jnp.logical_and(j >= 0, j < sent[direction])))
         return items
 
-    @pl.when(jnp.logical_or(z == 0, z == n_z - 1))
+    at_end = jnp.logical_or(z == 0, z == n_z - 1)
+
+    @pl.when(at_end)
     def _():
-        start_parts(n_z - 1 - z)
+        start_grads(n_z - 1 - z)
+
+    weight_copies[-1].wait()
+
+    @pl.when(at_end)
+    def _():
+        start_out(n_z - 1 - z)
 
     def step(s, carry):
         items = at_step(s)
@@ -608,7 +629,8 @@
 
             @pl.when(wanted)
             def _():
-                start_parts(part)
+                start_grads(part)
+                start_out(part)
 
             return c
 
@@ -726,9 +748,11 @@
             jax.ShapeDtypeStruct((tokens, feat), bf),
             jax.ShapeDtypeStruct((n_dp, shard // n_dp, enc), bf),
         ),
-        in_specs=[vm, vm, vm, hbm, hbm, hbm],
+        in_specs=[vm, hbm, hbm, hbm, hbm, hbm],
         out_specs=(vm, hbm),
         scratch_shapes=[
+            pltpu.VMEM(gk.shape, bf),
+            pltpu.VMEM(gv.shape, bf),
             pltpu.VMEM(w_key.shape, bf),
             pltpu.VMEM(w_value.shape, bf),
             pltpu.VMEM(w_out.shape, bf),
@@ -740,7 +764,7 @@
             pltpu.VMEM((n_z, tokens, feat), bf),
             pltpu.VMEM((n_z, tokens, feat), bf),
             pltpu.VMEM((n_z + 1, tokens, feat), bf),
-            dma((3,)),
+            dma((5,)),
             dma((n_z,)),
             dma((n_z,)),
             dma((n_z,)),
@@ -778,17 +802,15 @@
     position = jnp.where(slot_owner >= 0, dest_group * capacity + rank_in, -1)
     picked = position[None, :] == slot_order[:, None]
     source = jnp.sum(jnp.where(picked, slot_order[None, :], 0), axis=1)
-    filled = jnp.any(picked, axis=1)
-    send_rows = jnp.where(
-        filled[:, None, None], jnp.take(neighbours, source, axis=0), jnp.zeros((), jnp.bfloat16)
-    )
+    send_rows = neighbours.at[source].get(mode="promise_in_bounds")
     send_rows = send_rows.reshape(groups, capacity * rows_dev, enc_width)
     send_tags = jnp.sum(
         jnp.where(picked, slot_owner[None, :] + 1, 0), axis=1
     ).reshape(groups, capacity) - 1
     counts_rows = jnp.broadcast_to(counts[:, None], (spans, hidden_in.shape[0]))
     attended, grad_keys, grad_values = forward(
-        jnp.concatenate([hidden_in, out_grad], axis=0),
+        hidden_in,
+        out_grad,
         send_rows,
         send_tags,
         counts_rows,

time: 232 us -> 228 us (0.983)
  Pallas kernels: 222 us -> 218 us
    pallas_call x1, Pallas kernels: 121 us -> 117 us  [backward(): pl.pallas_call(functools.partial(backward_kernel, n_dp, n_mp), out_shape=...]
where the time goes in v4:
time: 228 us
  Pallas kernels  218 us (96%)
  local copies, waits for them, and re-layouts  6.25 us (3%)
  other arithmetic  2.9 us (1%)
    pallas_call x1, Pallas kernels, backward(): pl.pallas_call(functools.partial(backward_kernel, n_dp, n_mp), out_shape=...  117 us
    pallas_call x1, Pallas kernels, forward(): pl.pallas_call(functools.partial(forward_kernel, n_dp, n_mp, capacity), o...  101 us

profile of v4, /device:TPU:15, one launch (start us, length us, event | category | flops | bytes accessed | tf_op | source)
XLA Modules:
  0.0 227.7 jit_solution(1409008412104565834)
XLA Ops:
  0.6 0.0 copy-start
  0.6 0.8 fusion.2
  1.4 0.2 convert_reduce_fusion
  1.6 0.7 broadcast_compare_fusion
  2.2 0.1 select_reduce_fusion
  2.4 0.0 copy-done
  2.4 1.6 gather_fusion
  4.0 0.1 sub.11
  4.1 0.7 broadcast_in_dim.67.tags_in
  4.8 1.3 broadcast_in_dim.68.counts_in
  6.1 100.8 %gather_attend.1 = (bf16[128,512]{1,0:T(8,128)(2,1)}, bf16[8,320,512]{2,1,0:T(8,128)(2,1)}, bf16[8,320,512]{2,1,0:T(8,128)(2,1)}) custom-call(bf16[128,1024]{1,0:T(8,128)(2,1)} %x_in.1, bf16[128,1024]{1,0:T(8,128)(2,1)} %dy_in.1, bf16[4,80,1536]{2,1,0:T(8,128)(2,1)} %bitcast.6, s32[4,8,128]{2,1,0:T(8,128)} %broadcast_in_dim.67.tags_in, ...), custom_call_target="tpu_custom_call" | custom-call | tf_op jit(solution)/shard_map/gather_attend/pallas_call | solution.py:355
  106.9 117.1 %grads_scatter.1 = (bf16[128,1024]{1,0:T(8,128)(2,1)}, bf16[4,80,1536]{2,1,0:T(8,128)(2,1)}) custom-call(bf16[128,512]{1,0:T(8,128)(2,1)} %get-tuple-element.7.att, bf16[8,320,512]{2,1,0:T(8,128)(2,1)} %get-tuple-element.8.gk_in, bf16[8,320,512]{2,1,0:T(8,128)(2,1)} %get-tuple-element.9.gv_in, bf16[1536,512]{1,0:T(8,128)(2,1)} %wk_in.3, ...), custom_call_target="tpu_custom_call" | custom-call | tf_op jit(solution)/shard_map/grads_scatter/pallas_call | solution.py:745
  224.0 0.0 copy-start.1
  224.0 1.8 gather_fusion.1
  225.9 1.2 select_select_fusion
  227.0 0.0 copy-done.1
  227.0 0.7 copy.12
  (6 shorter events, 0.0 us)
Async XLA Ops:
  0.6 1.8 copy-start
  224.0 3.1 %copy-start.1 = (bf16[128,1024]{1,0:T(8,128)(2,1)S(1)}, bf16[128,1024]{1,0:T(8,128)(2,1)}, u32[]{:S(2)}) copy-start(bf16[128,1024]{1,0:T(8,128)(2,1)} %get-tuple-element.21) | copy-start | bytes 786436
